TPU v7x, 256 devices: a whole 4x4x8 slice. The times are simulated.
256 devices in a mesh: dom: 256 (over z, y, x, core).
Axes of the slice: x: 4, y: 4, z: 8, core: 2. Of those that a mesh axis runs over, the one named last changes fastest.
Arguments:
- dofs: float32 [9, 35, 32768], P(None, None, 'dom'), may hold values from -6 to 6
- star: float32 [3, 9, 9, 32768], P(None, None, None, 'dom'), may hold values from -0.8 to 0.8
- flux_local: float32 [4, 9, 9, 32768], P(None, None, None, 'dom'), may hold values from -0.2 to 0.2
- flux_neigh: float32 [4, 9, 9, 32768], P(None, None, None, 'dom'), may hold values from -0.2 to 0.2
- neighbour: int32 [4, 32768], P(None, 'dom'), may hold values from 0 to 32767, as said below
- neighbour_face: int32 [4, 32768], P(None, 'dom'), may hold values from 0 to 3, as said below
- orientation: int32 [4, 32768], P(None, 'dom'), may hold values from 0 to 2, as said below
- face_kind: int32 [4, 32768], P(None, 'dom'), may hold values from 0 to 2
- cluster: int32 [32768], P('dom'), may hold values from 0 to 2, as said below
- deriv_stiff: float32 [3, 35, 35], replicated, may hold values from -1 to 1
- update_stiff: float32 [3, 35, 35], replicated, may hold values from -0.3125 to 0.3125
- face_proj: float32 [4, 15, 35], replicated, may hold values from -1 to 1
- face_lift: float32 [4, 35, 15], replicated, may hold values from -1.5 to 1.5
- orient_map: float32 [3, 15, 15], replicated, may hold values from -1.5 to 1.5
Outputs:
- advanced: float32 [9, 35, 32768], P(None, None, 'dom')
Inputs may be any that keep to these rules, and one draw needn't show every extreme that they name: Each partition (a block of 128 consecutive elements) holds exactly 32 elements of cluster 0, 32 of cluster 1 and 64 of cluster 2. The face relation is symmetric: if face f of element e has neighbour n and neighbour_face g, then face g of n has neighbour e and neighbour_face f, with the same orientation. Across an interior face the neighbour lies in the same partition or in a partition one or two apart along the loop of partitions, wrapping at the ends. Two partitions one apart share at most 64 faces and two partitions two apart at most 32; both bounds are reached. A face of kind 1 or 2 names its own element and its own face. `neighbour_face`: see neighbour. `orientation`: equal on both sides of an interior face; 0 on faces of kinds 1 and 2.
All inputs are finite; a program needn't handle non-finite values.
Results may differ from a plain program's by a relative error of at most 0.0003.
Values sent between devices are 32-bit elements; how exact they have to be, the bound alone decides.
A program may use at most 128 MiB of HBM per device.

v0:
```python
import functools

import jax
import jax.numpy as jnp
from jax import lax
from jax.experimental import pallas as pl
from jax.experimental.pallas import tpu as pltpu
from jax.sharding import PartitionSpec as P

ELEM_DEV = 128
CAP_NEAR = 64
CAP_FAR = 32
QUANTITIES = 9
BASIS = 35
FACE_BASIS = 15
ORDER = 5
SLOTS = 4

LANES = 128
ROWS = 40
FROWS = 16
COLS = QUANTITIES * LANES
GROUPS = QUANTITIES * 2
FAR_GROUPS = 5
OFFSETS = (1, -1, 2, -2)
F32 = jnp.float32
BF16 = jnp.bfloat16
HIGHEST = lax.Precision.HIGHEST


def halves(value):
    high = value.astype(BF16).astype(F32)
    return high, value - high


def stacked(value):
    high, low = halves(value)
    tail = jnp.zeros((LANES - 3 * ROWS, value.shape[1]), F32)
    return jnp.concatenate([high, low, high, tail], axis=0).astype(BF16)


def widened(value):
    high, low = halves(value)
    return (high + pltpu.roll(high, ROWS, 1) + pltpu.roll(low, 2 * ROWS, 1)).astype(BF16)


def column_of(row):
    return jnp.broadcast_to(row, (LANES, LANES)).T


def dot(a, b):
    return jnp.dot(a, b, preferred_element_type=F32)


def kernel(
    devices,
    dofs, star, flux_local, flux_neigh, neighbour, neighbour_face, orientation, face_kind, cluster,
    deriv_stiff, update_stiff, face_proj, face_lift, orient_map,
    out,
    fields, start, integral, rhs, product, face_rhs, own_terms, spread, arrived, gathered,
    deriv_w, all_w, lift_w, pad_w, turn_w, tile_w, lift_pad,
    one_local, one_send, one_recv, flux_own,
    near_out, near_in, far_out, far_in, send_sem, recv_sem,
):
    me = lax.axis_index("dom")
    partners = [lax.rem(me + (off + devices), devices) for off in OFFSETS]
    barrier = pltpu.get_barrier_semaphore()
    for partner in partners:
        pl.semaphore_signal(
            barrier, inc=1, device_id=(partner,), device_id_type=pl.DeviceIdType.MESH
        )

    pad_w[...] = jnp.zeros_like(pad_w)
    turn_w[...] = jnp.zeros_like(turn_w)
    tile_w[...] = jnp.zeros_like(tile_w)
    lift_pad[...] = jnp.zeros_like(lift_pad)
    deriv_w[...] = jnp.zeros_like(deriv_w)
    all_w[...] = jnp.zeros_like(all_w)
    for d in range(3):
        pad_w[d * ROWS:d * ROWS + BASIS, 0:BASIS] = deriv_stiff[d]
        tile_w[d, 0:BASIS, 0:BASIS] = update_stiff[d]
    deriv_w[0:128, :] = widened(pad_w[0:128, :])
    for d in range(3):
        pad_w[256 + d * ROWS:256 + (d + 1) * ROWS, :] = tile_w[d].T[0:ROWS, :]
    for f in range(4):
        pad_w[192 + f * FROWS:192 + f * FROWS + FACE_BASIS, :] = jnp.zeros((FACE_BASIS, LANES), F32)
        pad_w[192 + f * FROWS:192 + f * FROWS + FACE_BASIS, 0:BASIS] = face_proj[f]
        lift_pad[f, 0:BASIS, 0:FACE_BASIS] = face_lift[f]
    for o in range(3):
        turn_w[o * FROWS:o * FROWS + FACE_BASIS, 0:FACE_BASIS] = orient_map[o]
    for f in range(4):
        own_rows = pad_w[192 + f * FROWS:192 + (f + 1) * FROWS, :]
        pad_w[f * 48:(f + 1) * 48, :] = jnp.dot(
            turn_w[...], own_rows, precision=HIGHEST, preferred_element_type=F32
        )
    all_w[...] = widened(pad_w[...])
    lift_all = lift_pad[0]
    for f in range(1, 4):
        lift_all = lift_all + pltpu.roll(lift_pad[f], f * FROWS, 1)
    lift_high, lift_low = halves(lift_all)
    lift_w[:, 0:LANES] = (lift_high + pltpu.roll(lift_high, 64, 1)).astype(BF16)
    lift_w[:, LANES:] = lift_low.astype(BF16)

    shape = (4, LANES)
    lane4 = lax.broadcasted_iota(jnp.int32, shape, 1)
    face4 = lax.broadcasted_iota(jnp.int32, shape, 0)
    nb = neighbour[...]
    nf = neighbour_face[...]
    kind = face_kind[...]
    local_id = nb & (ELEM_DEV - 1)
    distance = (nb >> 7) - me
    distance = jnp.where(distance < 0, distance + devices, distance)
    interior = kind == 0
    group = jnp.full(shape, 4, jnp.int32)
    for number, off in enumerate(OFFSETS):
        group = jnp.where(interior & (distance == off % devices), number, group)
    own_key = lane4 * 4 + face4
    far_key = local_id * 4 + nf
    key = jnp.where((group == 0) | (group == 2), own_key, far_key)
    low = (group * 1024).astype(F32)
    full_key = (group * 1024 + key).astype(F32)
    columns = [column_of(full_key[f:f + 1, :]) for f in range(4)]
    ranks = []
    for f in range(4):
        count = jnp.zeros((LANES, LANES), F32)
        for g in range(4):
            before = (columns[g] < full_key[f:f + 1, :]) & (columns[g] >= low[f:f + 1, :])
            count = count + jnp.where(before, 1.0, 0.0)
        ranks.append(jnp.sum(count, axis=0, keepdims=True))
    rank = jnp.concatenate(ranks, axis=0)
    base = jnp.where(group == 0, 0.0, jnp.where(group == 1, 64.0, jnp.where(group == 2, 128.0, 160.0)))
    place = jnp.where(group < 4, base + rank, -1.0)
    inside = interior & (distance == 0)
    source = jnp.where(inside, nf * LANES + local_id, -1).astype(F32)
    row512 = lax.broadcasted_iota(jnp.int32, (4 * LANES, LANES), 0).astype(F32)
    row256 = row512[0:2 * LANES, :]
    lane128 = lax.broadcasted_iota(jnp.int32, (LANES, LANES), 1).astype(F32)
    for f in range(4):
        cols = slice(f * LANES, (f + 1) * LANES)
        one_local[:, cols] = jnp.where(row512 == source[f:f + 1, :], 1.0, 0.0).astype(BF16)
        one_recv[:, cols] = jnp.where(row256 == place[f:f + 1, :], 1.0, 0.0).astype(BF16)
        place_col = column_of(place[f:f + 1, :])
        one_send[cols, 0:LANES] = jnp.where(place_col == lane128, 1.0, 0.0).astype(BF16)
        one_send[cols, LANES:] = jnp.where(place_col == lane128 + 128.0, 1.0, 0.0).astype(BF16)

    mirror = jnp.where(
        lax.broadcasted_iota(jnp.int32, (QUANTITIES, LANES), 0) < 6, -1.0, 1.0
    ).astype(F32)
    for f in range(4):
        factor = mirror * jnp.where(kind[f:f + 1, :] == 1, 1.0, 0.0)
        flux_own[f] = flux_local[f] + factor[None] * flux_neigh[f]

    fields[...] = jnp.zeros_like(fields)
    for q in range(QUANTITIES):
        fields[q, 0:BASIS, :] = dofs[q]
    start[...] = jnp.zeros_like(start)
    face_rhs[...] = jnp.zeros_like(face_rhs)
    pl.semaphore_wait(barrier, 4)

    span_low = jnp.left_shift(jnp.ones((1, LANES), jnp.int32), cluster[...]) - 1
    lane8 = lax.broadcasted_iota(jnp.int32, (8, LANES), 1)
    left = lane8 < 64
    quarter = lane8 // 32
    turned = [orientation[f:f + 1, :] for f in range(4)]

    def col(q):
        return pl.ds(pl.multiple_of(q * LANES, LANES), LANES)

    def contract(row, q_first, count):
        totals = [None] * count
        for d in range(3):
            for p in range(QUANTITIES):
                block = product[row + d * ROWS:row + (d + 1) * ROWS, p * LANES:(p + 1) * LANES]
                for i in range(count):
                    term = star[d, q_first + i, pl.ds(p, 1), :] * block
                    totals[i] = term if totals[i] is None else totals[i] + term
        return totals

    def slot_step(slot, carry):
        offset = span_low & slot
        below = offset.astype(F32)
        above = below + 1.0
        weights = []
        up, down = above, below
        scale = 1.0
        for degree in range(ORDER):
            scale = scale / (degree + 1)
            weights.append((up - down) * scale)
            up, down = up * above, down * below
        begins = offset == 0

        for q in range(QUANTITIES):
            first = jnp.where(begins, fields[q], start[q])
            start[q] = first
            integral[q] = weights[0] * first
            rhs[:, q * LANES:(q + 1) * LANES] = stacked(first)

        for degree in range(1, ORDER):
            product[0:128, :] = dot(deriv_w[...], rhs[...])

            def some(i, c, weight=weights[degree], last=degree == ORDER - 1):
                q_first = i * 3
                totals = contract(0, q_first, 3)
                for j in range(3):
                    q = q_first + j
                    term = -totals[j]
                    total = integral[q] + weight * term
                    if last:
                        rhs[:, col(q)] = stacked(total)
                    else:
                        integral[q] = total
                        rhs[:, col(q)] = stacked(term)
                return c

            lax.fori_loop(0, 3, some, 0)

        product[...] = dot(all_w[...], rhs[...])
        for f in range(4):
            for q in range(QUANTITIES):
                cols = slice(q * LANES, (q + 1) * LANES)
                r = f * 48
                value = jnp.where(
                    turned[f] == 0, product[r:r + 16, cols],
                    jnp.where(turned[f] == 1, product[r + 16:r + 32, cols], product[r + 32:r + 48, cols]),
                )
                high, lower = halves(value)
                spread[q * 16:(q + 1) * 16, f * LANES:(f + 1) * LANES] = high.astype(BF16)
                spread[144 + q * 16:144 + (q + 1) * 16, f * LANES:(f + 1) * LANES] = lower.astype(BF16)

        packed = dot(spread[...], one_send[...])
        packed = packed[0:144, :] + packed[144:288, :]
        near = [packed[r * 8:(r + 1) * 8, 0:LANES] for r in range(GROUPS)]
        far = [packed[r * 8:(r + 1) * 8, LANES:] for r in range(GROUPS)]
        for j in range(QUANTITIES):
            rows = slice(j * 8, (j + 1) * 8)
            near_out[slot, 0, rows, :] = jnp.where(left, near[2 * j], pltpu.roll(near[2 * j + 1], 64, 1))
            near_out[slot, 1, rows, :] = jnp.where(left, pltpu.roll(near[2 * j], 64, 1), near[2 * j + 1])
        for j in range(FAR_GROUPS):
            rows = slice(j * 8, (j + 1) * 8)
            for side in range(2):
                value = pltpu.roll(far[j], (-32 * side) % LANES, 1) if side else far[j]
                for c in range(1, 4):
                    r = j + FAR_GROUPS * c
                    if r < GROUPS:
                        shift = (32 * c - 32 * side) % LANES
                        moved = pltpu.roll(far[r], shift, 1) if shift else far[r]
                        value = jnp.where(quarter == c, moved, value)
                far_out[slot, side, rows, :] = value

        copies = []
        for number in range(4):
            here, there = (near_out, near_in) if number < 2 else (far_out, far_in)
            copies.append(pltpu.make_async_remote_copy(
                src_ref=here.at[slot, number % 2],
                dst_ref=there.at[slot, 1 - number % 2],
                send_sem=send_sem.at[slot, number],
                recv_sem=recv_sem.at[slot, number ^ 1],
                device_id=(partners[number],),
                device_id_type=pl.DeviceIdType.MESH,
            ))
        for copy in copies:
            copy.start()

        def volume(i, c):
            totals = contract(256, i * 3, 3)
            for j in range(3):
                fields[i * 3 + j] = fields[i * 3 + j] + totals[j]
            return c

        lax.fori_loop(0, 3, volume, 0)

        def own_part(f, c):
            row = pl.multiple_of(f * FROWS, FROWS)
            values = [product[pl.ds(pl.multiple_of(192 + row, FROWS), FROWS), p * LANES:(p + 1) * LANES]
                      for p in range(QUANTITIES)]
            for q in range(QUANTITIES):
                total = None
                for p in range(QUANTITIES):
                    term = flux_own[f, q, pl.ds(p, 1), :] * values[p]
                    total = term if total is None else total + term
                own_terms[pl.ds(row, FROWS), q * LANES:(q + 1) * LANES] = total
            return c

        lax.fori_loop(0, 4, own_part, 0)
        both = dot(spread[...], one_local[...])
        gathered[...] = both[0:144, :] + both[144:288, :]

        for number in range(4):
            copies[number].wait_recv()
        for j in range(QUANTITIES):
            rows = slice(j * 8, (j + 1) * 8)
            ahead, behind = near_in[slot, 0, rows, :], near_in[slot, 1, rows, :]
            even = jnp.where(left, ahead, pltpu.roll(behind, 64, 1))
            odd = jnp.where(left, pltpu.roll(ahead, 64, 1), behind)
            high, lower = halves(jnp.concatenate([even, odd], axis=0))
            arrived[j * 16:(j + 1) * 16, 0:LANES] = high.astype(BF16)
            arrived[144 + j * 16:144 + (j + 1) * 16, 0:LANES] = lower.astype(BF16)
        pieces = [None] * GROUPS
        for j in range(FAR_GROUPS):
            rows = slice(j * 8, (j + 1) * 8)
            ahead, behind = far_in[slot, 0, rows, :], far_in[slot, 1, rows, :]
            for c in range(4):
                r = j + FAR_GROUPS * c
                if r < GROUPS:
                    first = pltpu.roll(ahead, (-32 * c) % LANES, 1) if c else ahead
                    shift = (32 - 32 * c) % LANES
                    second = pltpu.roll(behind, shift, 1) if shift else behind
                    pieces[r] = jnp.where(quarter == 0, first, second)
        for j in range(QUANTITIES):
            high, lower = halves(jnp.concatenate([pieces[2 * j], pieces[2 * j + 1]], axis=0))
            arrived[j * 16:(j + 1) * 16, LANES:] = high.astype(BF16)
            arrived[144 + j * 16:144 + (j + 1) * 16, LANES:] = lower.astype(BF16)
        both = dot(arrived[...], one_recv[...])
        gathered[...] = gathered[...] + (both[0:144, :] + both[144:288, :])

        def outside_part(f, c):
            row = pl.multiple_of(f * FROWS, FROWS)
            values = [gathered[p * FROWS:(p + 1) * FROWS, col(f)] for p in range(QUANTITIES)]
            for q in range(QUANTITIES):
                cols = slice(q * LANES, (q + 1) * LANES)
                total = own_terms[pl.ds(row, FROWS), cols]
                for p in range(QUANTITIES):
                    total = total + flux_neigh[f, q, pl.ds(p, 1), :] * values[p]
                high, lower = halves(total)
                high = high.astype(BF16)
                face_rhs[pl.ds(row, FROWS), cols] = high
                face_rhs[pl.ds(pl.multiple_of(row + 64, FROWS), FROWS), cols] = lower.astype(BF16)
                face_rhs[pl.ds(pl.multiple_of(row + 128, FROWS), FROWS), cols] = high
            return c

        lax.fori_loop(0, 4, outside_part, 0)
        lifted = dot(lift_w[...], face_rhs[...])
        for q in range(QUANTITIES):
            fields[q] = fields[q] - lifted[0:ROWS, q * LANES:(q + 1) * LANES]
        for copy in copies:
            copy.wait_send()
        return carry

    lax.fori_loop(0, SLOTS, slot_step, 0)
    for q in range(QUANTITIES):
        out[q] = fields[q, 0:BASIS, :]


def body(devices, *args):
    args = list(args)
    args[8] = args[8].reshape(1, -1)
    vmem = pl.BlockSpec(memory_space=pltpu.VMEM)
    scratch = [
        pltpu.VMEM((QUANTITIES, ROWS, LANES), F32),
        pltpu.VMEM((QUANTITIES, ROWS, LANES), F32),
        pltpu.VMEM((QUANTITIES, ROWS, LANES), F32),
        pltpu.VMEM((LANES, COLS), BF16),
        pltpu.VMEM((384, COLS), F32),
        pltpu.VMEM((256, COLS), BF16),
        pltpu.VMEM((4 * FROWS, COLS), F32),
        pltpu.VMEM((288, 512), BF16),
        pltpu.VMEM((288, 256), BF16),
        pltpu.VMEM((144, 512), F32),
        pltpu.VMEM((128, LANES), BF16),
        pltpu.VMEM((384, LANES), BF16),
        pltpu.VMEM((ROWS, 2 * LANES), BF16),
        pltpu.VMEM((384, LANES), F32),
        pltpu.VMEM((48, FROWS), F32),
        pltpu.VMEM((3, LANES, LANES), F32),
        pltpu.VMEM((4, ROWS, LANES), F32),
        pltpu.VMEM((512, 512), BF16),
        pltpu.VMEM((512, 256), BF16),
        pltpu.VMEM((256, 512), BF16),
        pltpu.VMEM((4, QUANTITIES, QUANTITIES, LANES), F32),
        pltpu.VMEM((SLOTS, 2, QUANTITIES * 8, LANES), F32),
        pltpu.VMEM((SLOTS, 2, QUANTITIES * 8, LANES), F32),
        pltpu.VMEM((SLOTS, 2, FAR_GROUPS * 8, LANES), F32),
        pltpu.VMEM((SLOTS, 2, FAR_GROUPS * 8, LANES), F32),
        pltpu.SemaphoreType.DMA((SLOTS, 4)),
        pltpu.SemaphoreType.DMA((SLOTS, 4)),
    ]
    return pl.pallas_call(
        functools.partial(kernel, devices),
        out_shape=jax.ShapeDtypeStruct(args[0].shape, F32),
        in_specs=[vmem] * len(args),
        out_specs=vmem,
        scratch_shapes=scratch,
        compiler_params=pltpu.CompilerParams(
            collective_id=0, has_side_effects=True, vmem_limit_bytes=40 * 2**20
        ),
    )(*args)


def solution(mesh):
    in_specs = (
        P(None, None, "dom"),
        P(None, None, None, "dom"),
        P(None, None, None, "dom"),
        P(None, None, None, "dom"),
        P(None, "dom"),
        P(None, "dom"),
        P(None, "dom"),
        P(None, "dom"),
        P("dom"),
        P(),
        P(),
        P(),
        P(),
        P(),
    )
    return jax.shard_map(
        functools.partial(body, mesh.shape["dom"]),
        mesh=mesh, in_specs=in_specs, out_specs=P(None, None, "dom"), check_vma=False,
    )
```

profile of v0, /device:TPU:1, one launch (start us, length us, event | category | flops | bytes accessed | tf_op | source)
XLA Modules:
  0.0 56.9 jit_solution(16652937879625843214)
XLA Ops:
  0.0 0.0 copy-start.11
  0.0 0.8 %copy.18.face_proj = f32[4,15,35]{2,1,0:T(8,128)S(1)} copy(f32[4,15,35]{2,0,1:T(4,128)} %param.25) | data formatting | bytes 16800 | tf_op args[11]
  0.8 0.9 %copy.19.face_lift = f32[4,35,15]{2,1,0:T(8,128)S(1)} copy(f32[4,35,15]{1,0,2:T(4,128)} %param.26) | data formatting | bytes 16800 | tf_op args[12]
  1.7 0.0 copy-done.11
  1.7 0.0 copy-start.9
  1.7 0.9 %copy-done.9 = f32[4,9,9,128]{3,0,2,1:T(4,128)S(1)} copy-done((f32[4,9,9,128]{3,0,2,1:T(4,128)S(1)}, f32[4,9,9,128]{3,0,2,1:T(4,128)}, u32[]{:S(2)}) %copy-start.9) | copy-done | bytes 165912
  2.6 0.0 copy-start.10
  2.6 0.9 %copy-done.10 = f32[4,9,9,128]{3,0,2,1:T(4,128)S(1)} copy-done((f32[4,9,9,128]{3,0,2,1:T(4,128)S(1)}, f32[4,9,9,128]{3,0,2,1:T(4,128)}, u32[]{:S(2)}) %copy-start.10) | copy-done | bytes 165912
  3.5 0.0 copy-start.4
  3.5 0.0 copy-start.5
  3.5 0.0 copy-start.6
  3.5 0.0 copy-start.7
  3.6 0.0 copy-start.8
  3.6 0.8 %copy-done = f32[9,35,128]{2,1,0:T(8,128)S(1)} copy-done((f32[9,35,128]{2,1,0:T(8,128)S(1)}, f32[9,35,128]{2,1,0:T(8,128)}, u32[]{:S(2)}) %copy-start) | copy-done | bytes 161304
  4.4 0.0 copy-done.1
  4.4 0.0 copy-done.2
  4.4 0.0 copy-done.3
  4.4 0.0 copy-done.4
  4.5 0.0 copy-done.5
  4.5 0.0 copy-done.6
  4.5 0.0 copy-done.7
  4.5 0.0 copy-done.8
  4.5 51.7 %shard_map.136 = f32[9,35,128]{2,1,0:T(8,128)S(1)} custom-call(f32[9,35,128]{2,1,0:T(8,128)S(1)} %copy-done, f32[3,9,9,128]{3,2,1,0:T(8,128)S(1)} %copy.15.star, f32[4,9,9,128]{3,2,1,0:T(8,128)S(1)} %copy.16.flux_local, f32[4,9,9,128]{3,2,1,0:T(8,128)S(1)} %copy.17.flux_neigh, s32[4,128]{1,0:T(4,128)S(1)} %copy-done.4, s32[4,128]{1,0:T(4,128)S(1)} %copy-done.5, ...), custom_call_target="tpu_custom_call" | custom-call | tf_op jit(solution)/shard_map/pallas_call | solution.py:377
  56.2 0.7 %copy.21 = f32[9,35,128]{2,1,0:T(8,128)} copy(f32[9,35,128]{2,1,0:T(8,128)S(1)} %shard_map.136) | data formatting | bytes 322560
  (7 shorter events, 0.1 us)
Async XLA Ops:
  0.0 1.7 %copy-start.11 = (f32[3,9,9,128]{3,0,2,1:T(4,128)S(1)}, f32[3,9,9,128]{3,0,2,1:T(4,128)}, u32[]{:S(2)}) copy-start(f32[3,9,9,128]{3,0,2,1:T(4,128)} %param.15) | copy-start | bytes 373252
  1.7 0.9 %copy-start.9 = (f32[4,9,9,128]{3,0,2,1:T(4,128)S(1)}, f32[4,9,9,128]{3,0,2,1:T(4,128)}, u32[]{:S(2)}) copy-start(f32[4,9,9,128]{3,0,2,1:T(4,128)} %param.16) | copy-start | bytes 497668
  2.6 0.9 %copy-start.10 = (f32[4,9,9,128]{3,0,2,1:T(4,128)S(1)}, f32[4,9,9,128]{3,0,2,1:T(4,128)}, u32[]{:S(2)}) copy-start(f32[4,9,9,128]{3,0,2,1:T(4,128)} %param.17) | copy-start | bytes 497668
  3.5 0.9 %copy-start = (f32[9,35,128]{2,1,0:T(8,128)S(1)}, f32[9,35,128]{2,1,0:T(8,128)}, u32[]{:S(2)}) copy-start(f32[9,35,128]{2,1,0:T(8,128)} %dofs.1) | copy-start | bytes 483844
  3.5 0.9 %copy-start.1 = (f32[3,35,35]{2,1,0:T(8,128)S(1)}, f32[3,35,35]{2,1,0:T(8,128)}, u32[]{:S(2)}) copy-start(f32[3,35,35]{2,1,0:T(8,128)} %deriv_stiff.1) | copy-start | bytes 44104
  3.5 0.9 %copy-start.2 = (f32[3,35,35]{2,1,0:T(8,128)S(1)}, f32[3,35,35]{2,1,0:T(8,128)}, u32[]{:S(2)}) copy-start(f32[3,35,35]{2,1,0:T(8,128)} %update_stiff.1) | copy-start | bytes 44104
  3.5 0.9 %copy-start.3 = (f32[3,15,15]{2,1,0:T(8,128)S(1)}, f32[3,15,15]{2,1,0:T(8,128)}, u32[]{:S(2)}) copy-start(f32[3,15,15]{2,1,0:T(8,128)} %orient_map.1) | copy-start | bytes 8104
  3.5 0.9 %copy-start.4 = (s32[4,128]{1,0:T(4,128)S(1)}, s32[4,128]{1,0:T(4,128)}, u32[]{:S(2)}) copy-start(s32[4,128]{1,0:T(4,128)} %neighbour.1) | copy-start | bytes 6148
  3.5 0.9 %copy-start.5 = (s32[4,128]{1,0:T(4,128)S(1)}, s32[4,128]{1,0:T(4,128)}, u32[]{:S(2)}) copy-start(s32[4,128]{1,0:T(4,128)} %neighbour_face.1) | copy-start | bytes 6148
  3.5 0.9 %copy-start.6 = (s32[4,128]{1,0:T(4,128)S(1)}, s32[4,128]{1,0:T(4,128)}, u32[]{:S(2)}) copy-start(s32[4,128]{1,0:T(4,128)} %orientation.1) | copy-start | bytes 6148
  3.5 0.9 %copy-start.7 = (s32[4,128]{1,0:T(4,128)S(1)}, s32[4,128]{1,0:T(4,128)}, u32[]{:S(2)}) copy-start(s32[4,128]{1,0:T(4,128)} %face_kind.1) | copy-start | bytes 6148
  3.6 0.9 %copy-start.8 = (s32[128]{0:T(128)S(1)}, s32[128]{0:T(128)}, u32[]{:S(2)}) copy-start(s32[128]{0:T(128)} %param.22) | copy-start | bytes 1540
where the time goes:
time: 57.1 us; the launch traced here: 56.9 us
  Pallas kernels  51.7 us (91%)
  local copies, waits for them, and re-layouts  5.06 us (9%)
    pallas_call x1, Pallas kernels, body(): pl.pallas_call(functools.partial(kernel, devices), out_shape=jax.ShapeDty...  51.7 us
    unnamed x30, local copies, waits for them, and re-layouts  5.06 us

commit v1 on v0

--- a/solution.py
+++ b/solution.py
@@ -52,16 +52,28 @@
     return jnp.dot(a, b, preferred_element_type=F32)
 
 
-def kernel(
-    devices,
-    dofs, star, flux_local, flux_neigh, neighbour, neighbour_face, orientation, face_kind, cluster,
-    deriv_stiff, update_stiff, face_proj, face_lift, orient_map,
-    out,
-    fields, start, integral, rhs, product, face_rhs, own_terms, spread, arrived, gathered,
-    deriv_w, all_w, lift_w, pad_w, turn_w, tile_w, lift_pad,
-    one_local, one_send, one_recv, flux_own,
-    near_out, near_in, far_out, far_in, send_sem, recv_sem,
-):
+def kernel(devices, *refs):
+    operands, out, landed, (
+        fields, start, integral, rhs, product, face_rhs, own_terms, spread, arrived, gathered,
+        deriv_w, all_w, lift_w, pad_w, turn_w, tile_w,
+        one_local, one_send, one_recv, where_from, flux_own,
+        near_out, near_in, far_out, far_in, send_sem, recv_sem,
+        in_sem,
+    ) = refs[:14], refs[14], refs[15:29], refs[29:]
+    (
+        dofs, star, flux_local, flux_neigh, neighbour, neighbour_face, orientation, face_kind, cluster,
+        deriv_stiff, update_stiff, face_proj, face_lift, orient_map,
+    ) = landed
+    loads = [
+        pltpu.make_async_copy(operands[number], landed[number], in_sem.at[number])
+        for number in range(14)
+    ]
+    first_loads = (4, 5, 7, 11, 13, 9, 10)
+    then_loads = (8, 0, 1)
+    late_loads = (6, 12, 2, 3)
+    for number in first_loads + then_loads + late_loads:
+        loads[number].start()
+
     me = lax.axis_index("dom")
     partners = [lax.rem(me + (off + devices), devices) for off in OFFSETS]
     barrier = pltpu.get_barrier_semaphore()
@@ -73,9 +85,13 @@
     pad_w[...] = jnp.zeros_like(pad_w)
     turn_w[...] = jnp.zeros_like(turn_w)
     tile_w[...] = jnp.zeros_like(tile_w)
-    lift_pad[...] = jnp.zeros_like(lift_pad)
     deriv_w[...] = jnp.zeros_like(deriv_w)
     all_w[...] = jnp.zeros_like(all_w)
+    fields[...] = jnp.zeros_like(fields)
+    start[...] = jnp.zeros_like(start)
+    face_rhs[...] = jnp.zeros_like(face_rhs)
+    for number in first_loads:
+        loads[number].wait()
     for d in range(3):
         pad_w[d * ROWS:d * ROWS + BASIS, 0:BASIS] = deriv_stiff[d]
         tile_w[d, 0:BASIS, 0:BASIS] = update_stiff[d]
@@ -83,23 +99,17 @@
     for d in range(3):
         pad_w[256 + d * ROWS:256 + (d + 1) * ROWS, :] = tile_w[d].T[0:ROWS, :]
     for f in range(4):
-        pad_w[192 + f * FROWS:192 + f * FROWS + FACE_BASIS, :] = jnp.zeros((FACE_BASIS, LANES), F32)
-        pad_w[192 + f * FROWS:192 + f * FROWS + FACE_BASIS, 0:BASIS] = face_proj[f]
-        lift_pad[f, 0:BASIS, 0:FACE_BASIS] = face_lift[f]
+        pad_w[192 + f * FROWS:192 + (f + 1) * FROWS, :] = jnp.zeros((FROWS, LANES), F32)
+        pad_w[192 + f * FROWS:192 + f * FROWS + FACE_BASIS, 0:BASIS] = face_proj[:, f, :]
     for o in range(3):
         turn_w[o * FROWS:o * FROWS + FACE_BASIS, 0:FACE_BASIS] = orient_map[o]
+    own_rows = jnp.concatenate(
+        [pad_w[192 + f * FROWS:192 + (f + 1) * FROWS, :] for f in range(4)], axis=1
+    )
+    turned_rows = jnp.dot(turn_w[...], own_rows, precision=HIGHEST, preferred_element_type=F32)
     for f in range(4):
-        own_rows = pad_w[192 + f * FROWS:192 + (f + 1) * FROWS, :]
-        pad_w[f * 48:(f + 1) * 48, :] = jnp.dot(
-            turn_w[...], own_rows, precision=HIGHEST, preferred_element_type=F32
-        )
+        pad_w[f * 48:(f + 1) * 48, :] = turned_rows[:, f * LANES:(f + 1) * LANES]
     all_w[...] = widened(pad_w[...])
-    lift_all = lift_pad[0]
-    for f in range(1, 4):
-        lift_all = lift_all + pltpu.roll(lift_pad[f], f * FROWS, 1)
-    lift_high, lift_low = halves(lift_all)
-    lift_w[:, 0:LANES] = (lift_high + pltpu.roll(lift_high, 64, 1)).astype(BF16)
-    lift_w[:, LANES:] = lift_low.astype(BF16)
 
     shape = (4, LANES)
     lane4 = lax.broadcasted_iota(jnp.int32, shape, 1)
@@ -132,29 +142,38 @@
     place = jnp.where(group < 4, base + rank, -1.0)
     inside = interior & (distance == 0)
     source = jnp.where(inside, nf * LANES + local_id, -1).astype(F32)
-    row512 = lax.broadcasted_iota(jnp.int32, (4 * LANES, LANES), 0).astype(F32)
-    row256 = row512[0:2 * LANES, :]
     lane128 = lax.broadcasted_iota(jnp.int32, (LANES, LANES), 1).astype(F32)
     for f in range(4):
         cols = slice(f * LANES, (f + 1) * LANES)
-        one_local[:, cols] = jnp.where(row512 == source[f:f + 1, :], 1.0, 0.0).astype(BF16)
-        one_recv[:, cols] = jnp.where(row256 == place[f:f + 1, :], 1.0, 0.0).astype(BF16)
         place_col = column_of(place[f:f + 1, :])
         one_send[cols, 0:LANES] = jnp.where(place_col == lane128, 1.0, 0.0).astype(BF16)
         one_send[cols, LANES:] = jnp.where(place_col == lane128 + 128.0, 1.0, 0.0).astype(BF16)
-
-    mirror = jnp.where(
-        lax.broadcasted_iota(jnp.int32, (QUANTITIES, LANES), 0) < 6, -1.0, 1.0
-    ).astype(F32)
-    for f in range(4):
-        factor = mirror * jnp.where(kind[f:f + 1, :] == 1, 1.0, 0.0)
-        flux_own[f] = flux_local[f] + factor[None] * flux_neigh[f]
-
-    fields[...] = jnp.zeros_like(fields)
+    where_from[0] = source
+    where_from[1] = place
+
+    def late_setup():
+        row512 = lax.broadcasted_iota(jnp.int32, (4 * LANES, LANES), 0).astype(F32)
+        row256 = row512[0:2 * LANES, :]
+        for f in range(4):
+            cols = slice(f * LANES, (f + 1) * LANES)
+            one_local[:, cols] = jnp.where(row512 == where_from[0, f:f + 1, :], 1.0, 0.0).astype(BF16)
+            one_recv[:, cols] = jnp.where(row256 == where_from[1, f:f + 1, :], 1.0, 0.0).astype(BF16)
+        mirror = jnp.where(
+            lax.broadcasted_iota(jnp.int32, (QUANTITIES, 4, LANES), 0) < 6, -1.0, 1.0
+        ).astype(F32)
+        factor = mirror * jnp.where(face_kind[...] == 1, 1.0, 0.0)[None]
+        for q in range(QUANTITIES):
+            flux_own[q] = flux_local[q] + factor * flux_neigh[q]
+        for f in range(4):
+            tile_w[3, f * FROWS:f * FROWS + FACE_BASIS, 0:BASIS] = face_lift[:, f, :]
+        lift_high, lift_low = halves(tile_w[3].T[0:ROWS, :])
+        lift_w[:, 0:LANES] = (lift_high + pltpu.roll(lift_high, 64, 1)).astype(BF16)
+        lift_w[:, LANES:] = lift_low.astype(BF16)
+
+    for number in then_loads + late_loads:
+        loads[number].wait()
     for q in range(QUANTITIES):
         fields[q, 0:BASIS, :] = dofs[q]
-    start[...] = jnp.zeros_like(start)
-    face_rhs[...] = jnp.zeros_like(face_rhs)
     pl.semaphore_wait(barrier, 4)
 
     span_low = jnp.left_shift(jnp.ones((1, LANES), jnp.int32), cluster[...]) - 1
@@ -172,7 +191,7 @@
             for p in range(QUANTITIES):
                 block = product[row + d * ROWS:row + (d + 1) * ROWS, p * LANES:(p + 1) * LANES]
                 for i in range(count):
-                    term = star[d, q_first + i, pl.ds(p, 1), :] * block
+                    term = star[q_first + i, p, d:d + 1, :] * block
                     totals[i] = term if totals[i] is None else totals[i] + term
         return totals
 
@@ -261,6 +280,7 @@
         for copy in copies:
             copy.start()
 
+        pl.when(slot == 0)(late_setup)
         def volume(i, c):
             totals = contract(256, i * 3, 3)
             for j in range(3):
@@ -276,7 +296,7 @@
             for q in range(QUANTITIES):
                 total = None
                 for p in range(QUANTITIES):
-                    term = flux_own[f, q, pl.ds(p, 1), :] * values[p]
+                    term = flux_own[q, p, pl.ds(f, 1), :] * values[p]
                     total = term if total is None else total + term
                 own_terms[pl.ds(row, FROWS), q * LANES:(q + 1) * LANES] = total
             return c
@@ -320,7 +340,7 @@
                 cols = slice(q * LANES, (q + 1) * LANES)
                 total = own_terms[pl.ds(row, FROWS), cols]
                 for p in range(QUANTITIES):
-                    total = total + flux_neigh[f, q, pl.ds(p, 1), :] * values[p]
+                    total = total + flux_neigh[q, p, pl.ds(f, 1), :] * values[p]
                 high, lower = halves(total)
                 high = high.astype(BF16)
                 face_rhs[pl.ds(row, FROWS), cols] = high
@@ -344,8 +364,13 @@
 def body(devices, *args):
     args = list(args)
     args[8] = args[8].reshape(1, -1)
+    for number in (1, 2, 3):
+        args[number] = jnp.transpose(args[number], (1, 2, 0, 3))
+    args[11] = jnp.transpose(args[11], (1, 0, 2))
+    args[12] = jnp.transpose(args[12], (2, 0, 1))
     vmem = pl.BlockSpec(memory_space=pltpu.VMEM)
-    scratch = [
+    hbm = pl.BlockSpec(memory_space=pltpu.HBM)
+    scratch = [pltpu.VMEM(arg.shape, arg.dtype) for arg in args] + [
         pltpu.VMEM((QUANTITIES, ROWS, LANES), F32),
         pltpu.VMEM((QUANTITIES, ROWS, LANES), F32),
         pltpu.VMEM((QUANTITIES, ROWS, LANES), F32),
@@ -361,23 +386,25 @@
         pltpu.VMEM((ROWS, 2 * LANES), BF16),
         pltpu.VMEM((384, LANES), F32),
         pltpu.VMEM((48, FROWS), F32),
-        pltpu.VMEM((3, LANES, LANES), F32),
-        pltpu.VMEM((4, ROWS, LANES), F32),
+        pltpu.VMEM((4, LANES, LANES), F32),
         pltpu.VMEM((512, 512), BF16),
         pltpu.VMEM((512, 256), BF16),
         pltpu.VMEM((256, 512), BF16),
-        pltpu.VMEM((4, QUANTITIES, QUANTITIES, LANES), F32),
+        pltpu.VMEM((2, 4, LANES), F32),
+        pltpu.VMEM((QUANTITIES, QUANTITIES, 4, LANES), F32),
         pltpu.VMEM((SLOTS, 2, QUANTITIES * 8, LANES), F32),
         pltpu.VMEM((SLOTS, 2, QUANTITIES * 8, LANES), F32),
         pltpu.VMEM((SLOTS, 2, FAR_GROUPS * 8, LANES), F32),
         pltpu.VMEM((SLOTS, 2, FAR_GROUPS * 8, LANES), F32),
         pltpu.SemaphoreType.DMA((SLOTS, 4)),
         pltpu.SemaphoreType.DMA((SLOTS, 4)),
+        pltpu.SemaphoreType.DMA((14,)),
     ]
+    args = [pltpu.with_memory_space_constraint(arg, pltpu.HBM) for arg in args]
     return pl.pallas_call(
         functools.partial(kernel, devices),
         out_shape=jax.ShapeDtypeStruct(args[0].shape, F32),
-        in_specs=[vmem] * len(args),
+        in_specs=[hbm] * len(args),
         out_specs=vmem,
         scratch_shapes=scratch,
         compiler_params=pltpu.CompilerParams(

time: 57.1 us -> 52.4 us (0.918)
  local copies, waits for them, and re-layouts: 5.06 us -> 0.68 us
    unnamed x30 -> x1, local copies, waits for them, and re-layouts: 5.06 us -> 0.68 us
where the time goes in v1:
time: 52.4 us; the launch traced here: 52.3 us
  Pallas kernels  51.7 us (99%)
  local copies, waits for them, and re-layouts  0.68 us (1%)
    pallas_call x1, Pallas kernels, body(): pl.pallas_call(functools.partial(kernel, devices), out_shape=jax.ShapeDty...  51.7 us

profile of v1, /device:TPU:1, one launch (start us, length us, event | category | flops | bytes accessed | tf_op | source)
XLA Modules:
  0.0 52.3 jit_solution(9342062396056903106)
XLA Ops:
  0.0 51.7 %shard_map.136 = f32[9,35,128]{2,1,0:T(8,128)S(1)} custom-call(f32[9,35,128]{2,1,0:T(8,128)} %refs_0_.1, f32[9,9,3,128]{3,2,1,0:T(4,128)} %bitcast.6, f32[9,9,4,128]{3,2,1,0:T(4,128)} %bitcast.7, f32[9,9,4,128]{3,2,1,0:T(4,128)} %bitcast.8, s32[4,128]{1,0:T(4,128)} %refs_4_.1, s32[4,128]{1,0:T(4,128)} %refs_5_.1, s32[4,128]{1,0:T(4,128)} %refs_6_.1, ...), custom_call_target="tpu_custom_call" | custom-call | tf_op jit(solution)/shard_map/pallas_call | solution.py:404
  51.7 0.7 %copy.16 = f32[9,35,128]{2,1,0:T(8,128)} copy(f32[9,35,128]{2,1,0:T(8,128)S(1)} %shard_map.136) | data formatting | bytes 322560

commit v2 on v1

--- a/solution.py
+++ b/solution.py
@@ -183,12 +183,12 @@
     turned = [orientation[f:f + 1, :] for f in range(4)]
 
     def col(q):
-        return pl.ds(pl.multiple_of(q * LANES, LANES), LANES)
+        return pl.ds(q * LANES, LANES)
 
     def contract(row, q_first, count):
         totals = [None] * count
-        for d in range(3):
-            for p in range(QUANTITIES):
+        for p in range(QUANTITIES):
+            for d in range(3):
                 block = product[row + d * ROWS:row + (d + 1) * ROWS, p * LANES:(p + 1) * LANES]
                 for i in range(count):
                     term = star[q_first + i, p, d:d + 1, :] * block
@@ -215,7 +215,9 @@
             rhs[:, q * LANES:(q + 1) * LANES] = stacked(first)
 
         for degree in range(1, ORDER):
-            product[0:128, :] = dot(deriv_w[...], rhs[...])
+            for tile in range(0, COLS, 256):
+                stop = min(tile + 256, COLS)
+                product[0:128, tile:stop] = dot(deriv_w[...], rhs[:, tile:stop])
 
             def some(i, c, weight=weights[degree], last=degree == ORDER - 1):
                 q_first = i * 3
@@ -231,7 +233,8 @@
                         rhs[:, col(q)] = stacked(term)
                 return c
 
-            lax.fori_loop(0, 3, some, 0)
+            for block in range(3):
+                some(block, 0)
 
         product[...] = dot(all_w[...], rhs[...])
         for f in range(4):
@@ -287,11 +290,12 @@
                 fields[i * 3 + j] = fields[i * 3 + j] + totals[j]
             return c
 
-        lax.fori_loop(0, 3, volume, 0)
+        for block in range(3):
+            volume(block, 0)
 
         def own_part(f, c):
-            row = pl.multiple_of(f * FROWS, FROWS)
-            values = [product[pl.ds(pl.multiple_of(192 + row, FROWS), FROWS), p * LANES:(p + 1) * LANES]
+            row = f * FROWS
+            values = [product[pl.ds(192 + row, FROWS), p * LANES:(p + 1) * LANES]
                       for p in range(QUANTITIES)]
             for q in range(QUANTITIES):
                 total = None
@@ -301,7 +305,8 @@
                 own_terms[pl.ds(row, FROWS), q * LANES:(q + 1) * LANES] = total
             return c
 
-        lax.fori_loop(0, 4, own_part, 0)
+        for block in range(4):
+            own_part(block, 0)
         both = dot(spread[...], one_local[...])
         gathered[...] = both[0:144, :] + both[144:288, :]
 
@@ -334,7 +339,7 @@
         gathered[...] = gathered[...] + (both[0:144, :] + both[144:288, :])
 
         def outside_part(f, c):
-            row = pl.multiple_of(f * FROWS, FROWS)
+            row = f * FROWS
             values = [gathered[p * FROWS:(p + 1) * FROWS, col(f)] for p in range(QUANTITIES)]
             for q in range(QUANTITIES):
                 cols = slice(q * LANES, (q + 1) * LANES)
@@ -344,11 +349,12 @@
                 high, lower = halves(total)
                 high = high.astype(BF16)
                 face_rhs[pl.ds(row, FROWS), cols] = high
-                face_rhs[pl.ds(pl.multiple_of(row + 64, FROWS), FROWS), cols] = lower.astype(BF16)
-                face_rhs[pl.ds(pl.multiple_of(row + 128, FROWS), FROWS), cols] = high
+                face_rhs[pl.ds(row + 64, FROWS), cols] = lower.astype(BF16)
+                face_rhs[pl.ds(row + 128, FROWS), cols] = high
             return c
 
-        lax.fori_loop(0, 4, outside_part, 0)
+        for block in range(4):
+            outside_part(block, 0)
         lifted = dot(lift_w[...], face_rhs[...])
         for q in range(QUANTITIES):
             fields[q] = fields[q] - lifted[0:ROWS, q * LANES:(q + 1) * LANES]

time: 52.4 us -> 50.1 us (0.956)
  Pallas kernels: 51.7 us -> 49.3 us
    pallas_call x1, Pallas kernels: 51.7 us -> 49.3 us  [body(): pl.pallas_call(functools.partial(kernel, devices), out_shape=jax.ShapeDty...]
where the time goes in v2:
time: 50.1 us; the launch traced here: 50 us
  Pallas kernels  49.3 us (98%)
  local copies, waits for them, and re-layouts  0.68 us (1%)
    pallas_call x1, Pallas kernels, body(): pl.pallas_call(functools.partial(kernel, devices), out_shape=jax.ShapeDty...  49.3 us

profile of v2, /device:TPU:1, one launch (start us, length us, event | category | flops | bytes accessed | tf_op | source)
XLA Modules:
  0.0 50.0 jit_solution(6340746720827063828)
XLA Ops:
  0.0 49.3 %shard_map.136 = f32[9,35,128]{2,1,0:T(8,128)S(1)} custom-call(f32[9,35,128]{2,1,0:T(8,128)} %refs_0_.1, f32[9,9,3,128]{3,2,1,0:T(4,128)} %bitcast.6, f32[9,9,4,128]{3,2,1,0:T(4,128)} %bitcast.7, f32[9,9,4,128]{3,2,1,0:T(4,128)} %bitcast.8, s32[4,128]{1,0:T(4,128)} %refs_4_.1, s32[4,128]{1,0:T(4,128)} %refs_5_.1, s32[4,128]{1,0:T(4,128)} %refs_6_.1, ...), custom_call_target="tpu_custom_call" | custom-call | tf_op jit(solution)/shard_map/pallas_call | solution.py:410
  49.3 0.7 %copy.16 = f32[9,35,128]{2,1,0:T(8,128)} copy(f32[9,35,128]{2,1,0:T(8,128)S(1)} %shard_map.136) | data formatting | bytes 322560

commit v3 on v1

--- a/solution.py
+++ b/solution.py
@@ -23,6 +23,7 @@
 GROUPS = QUANTITIES * 2
 FAR_GROUPS = 5
 OFFSETS = (1, -1, 2, -2)
+BLOCKS = ((0, 1, 2, 3), (4, 5, 6, 7), (8,))
 F32 = jnp.float32
 BF16 = jnp.bfloat16
 HIGHEST = lax.Precision.HIGHEST
@@ -54,7 +55,7 @@
 
 def kernel(devices, *refs):
     operands, out, landed, (
-        fields, start, integral, rhs, product, face_rhs, own_terms, spread, arrived, gathered,
+        fields, start, integral, rhs, first_z, second_z, turned_out, own_out, face_rhs, own_terms, spread, arrived, gathered,
         deriv_w, all_w, lift_w, pad_w, turn_w, tile_w,
         one_local, one_send, one_recv, where_from, flux_own,
         near_out, near_in, far_out, far_in, send_sem, recv_sem,
@@ -68,10 +69,9 @@
         pltpu.make_async_copy(operands[number], landed[number], in_sem.at[number])
         for number in range(14)
     ]
-    first_loads = (4, 5, 7, 11, 13, 9, 10)
-    then_loads = (8, 0, 1)
-    late_loads = (6, 12, 2, 3)
-    for number in first_loads + then_loads + late_loads:
+    first_loads = (9, 0, 1, 8, 4, 5, 7, 11, 13, 10, 6)
+    late_loads = (12, 2, 3)
+    for number in first_loads + late_loads:
         loads[number].start()
 
     me = lax.axis_index("dom")
@@ -152,6 +152,8 @@
     where_from[1] = place
 
     def late_setup():
+        for number in late_loads:
+            loads[number].wait()
         row512 = lax.broadcasted_iota(jnp.int32, (4 * LANES, LANES), 0).astype(F32)
         row256 = row512[0:2 * LANES, :]
         for f in range(4):
@@ -170,11 +172,8 @@
         lift_w[:, 0:LANES] = (lift_high + pltpu.roll(lift_high, 64, 1)).astype(BF16)
         lift_w[:, LANES:] = lift_low.astype(BF16)
 
-    for number in then_loads + late_loads:
-        loads[number].wait()
     for q in range(QUANTITIES):
         fields[q, 0:BASIS, :] = dofs[q]
-    pl.semaphore_wait(barrier, 4)
 
     span_low = jnp.left_shift(jnp.ones((1, LANES), jnp.int32), cluster[...]) - 1
     lane8 = lax.broadcasted_iota(jnp.int32, (8, LANES), 1)
@@ -182,20 +181,32 @@
     quarter = lane8 // 32
     turned = [orientation[f:f + 1, :] for f in range(4)]
 
+    def span_of(block):
+        return slice(block[0] * LANES, (block[-1] + 1) * LANES)
+
     def col(q):
-        return pl.ds(pl.multiple_of(q * LANES, LANES), LANES)
-
-    def contract(row, q_first, count):
-        totals = [None] * count
-        for d in range(3):
-            for p in range(QUANTITIES):
-                block = product[row + d * ROWS:row + (d + 1) * ROWS, p * LANES:(p + 1) * LANES]
-                for i in range(count):
-                    term = star[q_first + i, p, d:d + 1, :] * block
+        return slice(q * LANES, (q + 1) * LANES)
+
+    def contract(source_ref, row, block):
+        totals = [None] * len(block)
+        for p in range(QUANTITIES):
+            for d in range(3):
+                values = source_ref[row + d * ROWS:row + (d + 1) * ROWS, col(p)]
+                for i, q in enumerate(block):
+                    term = star[q, p, d:d + 1, :] * values
                     totals[i] = term if totals[i] is None else totals[i] + term
         return totals
 
-    def slot_step(slot, carry):
+    def face_contract(flux, source_ref, f, block, where):
+        totals = [None] * len(block)
+        for p in range(QUANTITIES):
+            values = source_ref[where(f, p)]
+            for i, q in enumerate(block):
+                term = flux[q, p, f:f + 1, :] * values
+                totals[i] = term if totals[i] is None else totals[i] + term
+        return totals
+
+    def slot_step(slot, carry, first_slot=False):
         offset = span_low & slot
         below = offset.astype(F32)
         above = below + 1.0
@@ -208,46 +219,49 @@
             up, down = up * above, down * below
         begins = offset == 0
 
-        for q in range(QUANTITIES):
-            first = jnp.where(begins, fields[q], start[q])
-            start[q] = first
-            integral[q] = weights[0] * first
-            rhs[:, q * LANES:(q + 1) * LANES] = stacked(first)
-
+        for block in BLOCKS:
+            for q in block:
+                first = fields[q] if first_slot else jnp.where(begins, fields[q], start[q])
+                start[q] = first
+                integral[q] = weights[0] * first
+                rhs[:, col(q)] = stacked(first)
+            first_z[:, span_of(block)] = dot(deriv_w[...], rhs[:, span_of(block)])
+
+        packed = []
         for degree in range(1, ORDER):
-            product[0:128, :] = dot(deriv_w[...], rhs[...])
-
-            def some(i, c, weight=weights[degree], last=degree == ORDER - 1):
-                q_first = i * 3
-                totals = contract(0, q_first, 3)
-                for j in range(3):
-                    q = q_first + j
-                    term = -totals[j]
-                    total = integral[q] + weight * term
+            z_now, z_next = (first_z, second_z) if degree % 2 else (second_z, first_z)
+            last = degree == ORDER - 1
+            for block in BLOCKS:
+                totals = contract(z_now, 0, block)
+                for q, total in zip(block, totals):
+                    term = -total
+                    sum_now = integral[q] + weights[degree] * term
                     if last:
-                        rhs[:, col(q)] = stacked(total)
+                        rhs[:, col(q)] = stacked(sum_now)
                     else:
-                        integral[q] = total
+                        integral[q] = sum_now
                         rhs[:, col(q)] = stacked(term)
-                return c
-
-            lax.fori_loop(0, 3, some, 0)
-
-        product[...] = dot(all_w[...], rhs[...])
-        for f in range(4):
-            for q in range(QUANTITIES):
-                cols = slice(q * LANES, (q + 1) * LANES)
-                r = f * 48
-                value = jnp.where(
-                    turned[f] == 0, product[r:r + 16, cols],
-                    jnp.where(turned[f] == 1, product[r + 16:r + 32, cols], product[r + 32:r + 48, cols]),
-                )
-                high, lower = halves(value)
-                spread[q * 16:(q + 1) * 16, f * LANES:(f + 1) * LANES] = high.astype(BF16)
-                spread[144 + q * 16:144 + (q + 1) * 16, f * LANES:(f + 1) * LANES] = lower.astype(BF16)
-
-        packed = dot(spread[...], one_send[...])
-        packed = packed[0:144, :] + packed[144:288, :]
+                cols = span_of(block)
+                if last:
+                    turned_out[:, cols] = dot(all_w[0:192, :], rhs[:, cols])
+                    for q in block:
+                        for f in range(4):
+                            r = f * 48
+                            value = jnp.where(
+                                turned[f] == 0, turned_out[r:r + 16, col(q)],
+                                jnp.where(turned[f] == 1, turned_out[r + 16:r + 32, col(q)],
+                                          turned_out[r + 32:r + 48, col(q)]),
+                            )
+                            high, lower = halves(value)
+                            spread[q * 32:q * 32 + 16, col(f)] = high.astype(BF16)
+                            spread[q * 32 + 16:q * 32 + 32, col(f)] = lower.astype(BF16)
+                    piece = dot(spread[block[0] * 32:(block[-1] + 1) * 32, :], one_send[...])
+                    for i in range(len(block)):
+                        packed.append(piece[i * 32:i * 32 + 16, :] + piece[i * 32 + 16:i * 32 + 32, :])
+                else:
+                    z_next[:, cols] = dot(deriv_w[...], rhs[:, cols])
+
+        packed = jnp.concatenate(packed, axis=0)
         near = [packed[r * 8:(r + 1) * 8, 0:LANES] for r in range(GROUPS)]
         far = [packed[r * 8:(r + 1) * 8, LANES:] for r in range(GROUPS)]
         for j in range(QUANTITIES):
@@ -266,6 +280,8 @@
                         value = jnp.where(quarter == c, moved, value)
                 far_out[slot, side, rows, :] = value
 
+        if first_slot:
+            pl.semaphore_wait(barrier, 4)
         copies = []
         for number in range(4):
             here, there = (near_out, near_in) if number < 2 else (far_out, far_in)
@@ -280,30 +296,24 @@
         for copy in copies:
             copy.start()
 
-        pl.when(slot == 0)(late_setup)
-        def volume(i, c):
-            totals = contract(256, i * 3, 3)
-            for j in range(3):
-                fields[i * 3 + j] = fields[i * 3 + j] + totals[j]
-            return c
-
-        lax.fori_loop(0, 3, volume, 0)
-
-        def own_part(f, c):
-            row = pl.multiple_of(f * FROWS, FROWS)
-            values = [product[pl.ds(pl.multiple_of(192 + row, FROWS), FROWS), p * LANES:(p + 1) * LANES]
-                      for p in range(QUANTITIES)]
-            for q in range(QUANTITIES):
-                total = None
-                for p in range(QUANTITIES):
-                    term = flux_own[q, p, pl.ds(f, 1), :] * values[p]
-                    total = term if total is None else total + term
-                own_terms[pl.ds(row, FROWS), q * LANES:(q + 1) * LANES] = total
-            return c
-
-        lax.fori_loop(0, 4, own_part, 0)
+        if first_slot:
+            late_setup()
         both = dot(spread[...], one_local[...])
-        gathered[...] = both[0:144, :] + both[144:288, :]
+        for q in range(QUANTITIES):
+            gathered[q * 16:q * 16 + 16, :] = both[q * 32:q * 32 + 16, :] + both[q * 32 + 16:q * 32 + 32, :]
+        for block in BLOCKS:
+            own_out[:, span_of(block)] = dot(all_w[192:384, :], rhs[:, span_of(block)])
+        for block in BLOCKS:
+            totals = contract(own_out, 64, block)
+            for q, total in zip(block, totals):
+                fields[q] = fields[q] + total
+        for f in range(4):
+            for block in BLOCKS:
+                totals = face_contract(
+                    flux_own, own_out, f, block, lambda f, p: (slice(f * FROWS, (f + 1) * FROWS), col(p))
+                )
+                for q, total in zip(block, totals):
+                    own_terms[f * FROWS:(f + 1) * FROWS, col(q)] = total
 
         for number in range(4):
             copies[number].wait_recv()
@@ -333,30 +343,28 @@
         both = dot(arrived[...], one_recv[...])
         gathered[...] = gathered[...] + (both[0:144, :] + both[144:288, :])
 
-        def outside_part(f, c):
-            row = pl.multiple_of(f * FROWS, FROWS)
-            values = [gathered[p * FROWS:(p + 1) * FROWS, col(f)] for p in range(QUANTITIES)]
-            for q in range(QUANTITIES):
-                cols = slice(q * LANES, (q + 1) * LANES)
-                total = own_terms[pl.ds(row, FROWS), cols]
-                for p in range(QUANTITIES):
-                    total = total + flux_neigh[q, p, pl.ds(f, 1), :] * values[p]
-                high, lower = halves(total)
-                high = high.astype(BF16)
-                face_rhs[pl.ds(row, FROWS), cols] = high
-                face_rhs[pl.ds(pl.multiple_of(row + 64, FROWS), FROWS), cols] = lower.astype(BF16)
-                face_rhs[pl.ds(pl.multiple_of(row + 128, FROWS), FROWS), cols] = high
-            return c
-
-        lax.fori_loop(0, 4, outside_part, 0)
-        lifted = dot(lift_w[...], face_rhs[...])
-        for q in range(QUANTITIES):
-            fields[q] = fields[q] - lifted[0:ROWS, q * LANES:(q + 1) * LANES]
+        for block in BLOCKS:
+            cols = span_of(block)
+            for f in range(4):
+                totals = face_contract(
+                    flux_neigh, gathered, f, block, lambda f, p: (slice(p * FROWS, (p + 1) * FROWS), col(f))
+                )
+                for q, total in zip(block, totals):
+                    row = f * FROWS
+                    high, lower = halves(own_terms[row:row + FROWS, col(q)] + total)
+                    high = high.astype(BF16)
+                    face_rhs[row:row + FROWS, col(q)] = high
+                    face_rhs[row + 64:row + 64 + FROWS, col(q)] = lower.astype(BF16)
+                    face_rhs[row + 128:row + 128 + FROWS, col(q)] = high
+            lifted = dot(lift_w[...], face_rhs[:, cols])
+            for i, q in enumerate(block):
+                fields[q] = fields[q] - lifted[0:ROWS, col(i)]
         for copy in copies:
             copy.wait_send()
         return carry
 
-    lax.fori_loop(0, SLOTS, slot_step, 0)
+    slot_step(0, 0, first_slot=True)
+    lax.fori_loop(1, SLOTS, slot_step, 0)
     for q in range(QUANTITIES):
         out[q] = fields[q, 0:BASIS, :]
 
@@ -375,7 +383,10 @@
         pltpu.VMEM((QUANTITIES, ROWS, LANES), F32),
         pltpu.VMEM((QUANTITIES, ROWS, LANES), F32),
         pltpu.VMEM((LANES, COLS), BF16),
-        pltpu.VMEM((384, COLS), F32),
+        pltpu.VMEM((128, COLS), F32),
+        pltpu.VMEM((128, COLS), F32),
+        pltpu.VMEM((192, COLS), F32),
+        pltpu.VMEM((192, COLS), F32),
         pltpu.VMEM((256, COLS), BF16),
         pltpu.VMEM((4 * FROWS, COLS), F32),
         pltpu.VMEM((288, 512), BF16),

time: 52.4 us -> 46.6 us (0.89)
  Pallas kernels: 51.7 us -> 45.8 us
    pallas_call x1, Pallas kernels: 51.7 us -> 45.8 us  [body(): pl.pallas_call(functools.partial(kernel, devices), out_shape=jax.ShapeDty...]
where the time goes in v3:
time: 46.6 us; the launch traced here: 46.5 us
  Pallas kernels  45.8 us (98%)
  local copies, waits for them, and re-layouts  0.68 us (1%)
    pallas_call x1, Pallas kernels, body(): pl.pallas_call(functools.partial(kernel, devices), out_shape=jax.ShapeDty...  45.8 us

profile of v3, /device:TPU:1, one launch (start us, length us, event | category | flops | bytes accessed | tf_op | source)
XLA Modules:
  0.0 46.5 jit_solution(561850407083769590)
XLA Ops:
  0.0 45.8 %shard_map.136 = f32[9,35,128]{2,1,0:T(8,128)S(1)} custom-call(f32[9,35,128]{2,1,0:T(8,128)} %refs_0_.1, f32[9,9,3,128]{3,2,1,0:T(4,128)} %bitcast.6, f32[9,9,4,128]{3,2,1,0:T(4,128)} %bitcast.7, f32[9,9,4,128]{3,2,1,0:T(4,128)} %bitcast.8, s32[4,128]{1,0:T(4,128)} %refs_4_.1, s32[4,128]{1,0:T(4,128)} %refs_5_.1, s32[4,128]{1,0:T(4,128)} %refs_6_.1, ...), custom_call_target="tpu_custom_call" | custom-call | tf_op jit(solution)/shard_map/pallas_call | solution.py:415
  45.8 0.7 %copy.16 = f32[9,35,128]{2,1,0:T(8,128)} copy(f32[9,35,128]{2,1,0:T(8,128)S(1)} %shard_map.136) | data formatting | bytes 322560

commit v4 on v3

--- a/solution.py
+++ b/solution.py
@@ -23,6 +23,7 @@
 GROUPS = QUANTITIES * 2
 FAR_GROUPS = 5
 OFFSETS = (1, -1, 2, -2)
+PARTS = ((range(0, 4), 0, 32, 0, 2), (range(4, 9), 32, 40, 16, 3))
 BLOCKS = ((0, 1, 2, 3), (4, 5, 6, 7), (8,))
 F32 = jnp.float32
 BF16 = jnp.bfloat16
@@ -206,6 +207,40 @@
                 totals[i] = term if totals[i] is None else totals[i] + term
         return totals
 
+    def send_part(slot, part, packed, copies):
+        members, near_row, near_rows, far_row, groups = PARTS[part]
+        first = 2 * members[0]
+        count = 2 * len(members)
+        for q in members:
+            rows = slice(q * 8, (q + 1) * 8)
+            even, odd = packed[q][0:8, 0:LANES], packed[q][8:16, 0:LANES]
+            near_out[slot, 0, rows, :] = jnp.where(left, even, pltpu.roll(odd, 64, 1))
+            near_out[slot, 1, rows, :] = jnp.where(left, pltpu.roll(even, 64, 1), odd)
+        far = [packed[(first + i) // 2][(i % 2) * 8:(i % 2) * 8 + 8, LANES:] for i in range(count)]
+        for j in range(groups):
+            rows = slice(far_row + j * 8, far_row + (j + 1) * 8)
+            for side in range(2):
+                value = pltpu.roll(far[j], 96, 1) if side else far[j]
+                for c in range(1, 4):
+                    if j + groups * c < count:
+                        shift = (32 * c - 32 * side) % LANES
+                        piece = far[j + groups * c]
+                        value = jnp.where(quarter == c, pltpu.roll(piece, shift, 1) if shift else piece, value)
+                far_out[slot, side, rows, :] = value
+        for number in range(4):
+            here, there = (near_out, near_in) if number < 2 else (far_out, far_in)
+            rows = pl.ds(near_row, near_rows) if number < 2 else pl.ds(far_row, groups * 8)
+            copy = pltpu.make_async_remote_copy(
+                src_ref=here.at[slot, number % 2, rows],
+                dst_ref=there.at[slot, 1 - number % 2, rows],
+                send_sem=send_sem.at[slot, part * 4 + number],
+                recv_sem=recv_sem.at[slot, part * 4 + (number ^ 1)],
+                device_id=(partners[number],),
+                device_id_type=pl.DeviceIdType.MESH,
+            )
+            copy.start()
+            copies.append(copy)
+
     def slot_step(slot, carry, first_slot=False):
         offset = span_low & slot
         below = offset.astype(F32)
@@ -228,6 +263,7 @@
             first_z[:, span_of(block)] = dot(deriv_w[...], rhs[:, span_of(block)])
 
         packed = []
+        copies = []
         for degree in range(1, ORDER):
             z_now, z_next = (first_z, second_z) if degree % 2 else (second_z, first_z)
             last = degree == ORDER - 1
@@ -258,43 +294,14 @@
                     piece = dot(spread[block[0] * 32:(block[-1] + 1) * 32, :], one_send[...])
                     for i in range(len(block)):
                         packed.append(piece[i * 32:i * 32 + 16, :] + piece[i * 32 + 16:i * 32 + 32, :])
+                    if block[-1] == PARTS[0][0][-1]:
+                        if first_slot:
+                            pl.semaphore_wait(barrier, 4)
+                        send_part(slot, 0, packed, copies)
                 else:
                     z_next[:, cols] = dot(deriv_w[...], rhs[:, cols])
 
-        packed = jnp.concatenate(packed, axis=0)
-        near = [packed[r * 8:(r + 1) * 8, 0:LANES] for r in range(GROUPS)]
-        far = [packed[r * 8:(r + 1) * 8, LANES:] for r in range(GROUPS)]
-        for j in range(QUANTITIES):
-            rows = slice(j * 8, (j + 1) * 8)
-            near_out[slot, 0, rows, :] = jnp.where(left, near[2 * j], pltpu.roll(near[2 * j + 1], 64, 1))
-            near_out[slot, 1, rows, :] = jnp.where(left, pltpu.roll(near[2 * j], 64, 1), near[2 * j + 1])
-        for j in range(FAR_GROUPS):
-            rows = slice(j * 8, (j + 1) * 8)
-            for side in range(2):
-                value = pltpu.roll(far[j], (-32 * side) % LANES, 1) if side else far[j]
-                for c in range(1, 4):
-                    r = j + FAR_GROUPS * c
-                    if r < GROUPS:
-                        shift = (32 * c - 32 * side) % LANES
-                        moved = pltpu.roll(far[r], shift, 1) if shift else far[r]
-                        value = jnp.where(quarter == c, moved, value)
-                far_out[slot, side, rows, :] = value
-
-        if first_slot:
-            pl.semaphore_wait(barrier, 4)
-        copies = []
-        for number in range(4):
-            here, there = (near_out, near_in) if number < 2 else (far_out, far_in)
-            copies.append(pltpu.make_async_remote_copy(
-                src_ref=here.at[slot, number % 2],
-                dst_ref=there.at[slot, 1 - number % 2],
-                send_sem=send_sem.at[slot, number],
-                recv_sem=recv_sem.at[slot, number ^ 1],
-                device_id=(partners[number],),
-                device_id_type=pl.DeviceIdType.MESH,
-            ))
-        for copy in copies:
-            copy.start()
+        send_part(slot, 1, packed, copies)
 
         if first_slot:
             late_setup()
@@ -315,34 +322,38 @@
                 for q, total in zip(block, totals):
                     own_terms[f * FROWS:(f + 1) * FROWS, col(q)] = total
 
-        for number in range(4):
-            copies[number].wait_recv()
-        for j in range(QUANTITIES):
-            rows = slice(j * 8, (j + 1) * 8)
-            ahead, behind = near_in[slot, 0, rows, :], near_in[slot, 1, rows, :]
-            even = jnp.where(left, ahead, pltpu.roll(behind, 64, 1))
-            odd = jnp.where(left, pltpu.roll(ahead, 64, 1), behind)
-            high, lower = halves(jnp.concatenate([even, odd], axis=0))
-            arrived[j * 16:(j + 1) * 16, 0:LANES] = high.astype(BF16)
-            arrived[144 + j * 16:144 + (j + 1) * 16, 0:LANES] = lower.astype(BF16)
-        pieces = [None] * GROUPS
-        for j in range(FAR_GROUPS):
-            rows = slice(j * 8, (j + 1) * 8)
-            ahead, behind = far_in[slot, 0, rows, :], far_in[slot, 1, rows, :]
-            for c in range(4):
-                r = j + FAR_GROUPS * c
-                if r < GROUPS:
-                    first = pltpu.roll(ahead, (-32 * c) % LANES, 1) if c else ahead
-                    shift = (32 - 32 * c) % LANES
-                    second = pltpu.roll(behind, shift, 1) if shift else behind
-                    pieces[r] = jnp.where(quarter == 0, first, second)
-        for j in range(QUANTITIES):
-            high, lower = halves(jnp.concatenate([pieces[2 * j], pieces[2 * j + 1]], axis=0))
-            arrived[j * 16:(j + 1) * 16, LANES:] = high.astype(BF16)
-            arrived[144 + j * 16:144 + (j + 1) * 16, LANES:] = lower.astype(BF16)
-        both = dot(arrived[...], one_recv[...])
-        gathered[...] = gathered[...] + (both[0:144, :] + both[144:288, :])
-
+        for part, (members, near_row, near_rows, far_row, groups) in enumerate(PARTS):
+            for number in range(4):
+                copies[part * 4 + number].wait_recv()
+            first = 2 * members[0]
+            count = 2 * len(members)
+            for q in members:
+                rows = slice(q * 8, (q + 1) * 8)
+                ahead, behind = near_in[slot, 0, rows, :], near_in[slot, 1, rows, :]
+                even = jnp.where(left, ahead, pltpu.roll(behind, 64, 1))
+                odd = jnp.where(left, pltpu.roll(ahead, 64, 1), behind)
+                high, lower = halves(jnp.concatenate([even, odd], axis=0))
+                arrived[q * 32:q * 32 + 16, 0:LANES] = high.astype(BF16)
+                arrived[q * 32 + 16:q * 32 + 32, 0:LANES] = lower.astype(BF16)
+            pieces = [None] * count
+            for j in range(groups):
+                rows = slice(far_row + j * 8, far_row + (j + 1) * 8)
+                ahead, behind = far_in[slot, 0, rows, :], far_in[slot, 1, rows, :]
+                for c in range(4):
+                    if j + groups * c < count:
+                        near_side = pltpu.roll(ahead, (-32 * c) % LANES, 1) if c else ahead
+                        shift = (32 - 32 * c) % LANES
+                        far_side = pltpu.roll(behind, shift, 1) if shift else behind
+                        pieces[j + groups * c] = jnp.where(quarter == 0, near_side, far_side)
+            for i, q in enumerate(members):
+                high, lower = halves(jnp.concatenate([pieces[2 * i], pieces[2 * i + 1]], axis=0))
+                arrived[q * 32:q * 32 + 16, LANES:] = high.astype(BF16)
+                arrived[q * 32 + 16:q * 32 + 32, LANES:] = lower.astype(BF16)
+            both = dot(arrived[members[0] * 32:(members[-1] + 1) * 32, :], one_recv[...])
+            for i, q in enumerate(members):
+                gathered[q * 16:(q + 1) * 16, :] = gathered[q * 16:(q + 1) * 16, :] + (
+                    both[i * 32:i * 32 + 16, :] + both[i * 32 + 16:i * 32 + 32, :]
+                )
         for block in BLOCKS:
             cols = span_of(block)
             for f in range(4):
@@ -407,8 +418,8 @@
         pltpu.VMEM((SLOTS, 2, QUANTITIES * 8, LANES), F32),
         pltpu.VMEM((SLOTS, 2, FAR_GROUPS * 8, LANES), F32),
         pltpu.VMEM((SLOTS, 2, FAR_GROUPS * 8, LANES), F32),
-        pltpu.SemaphoreType.DMA((SLOTS, 4)),
-        pltpu.SemaphoreType.DMA((SLOTS, 4)),
+        pltpu.SemaphoreType.DMA((SLOTS, 8)),
+        pltpu.SemaphoreType.DMA((SLOTS, 8)),
         pltpu.SemaphoreType.DMA((14,)),
     ]
     args = [pltpu.with_memory_space_constraint(arg, pltpu.HBM) for arg in args]

time: 46.6 us -> 47.3 us (1.015)
  Pallas kernels: 45.8 us -> 46.5 us
    pallas_call x1, Pallas kernels: 45.8 us -> 46.5 us  [body(): pl.pallas_call(functools.partial(kernel, devices), out_shape=jax.ShapeDty...]
where the time goes in v4:
time: 47.3 us; the launch traced here: 47.2 us
  Pallas kernels  46.5 us (98%)
  local copies, waits for them, and re-layouts  0.68 us (1%)
    pallas_call x1, Pallas kernels, body(): pl.pallas_call(functools.partial(kernel, devices), out_shape=jax.ShapeDty...  46.5 us

profile of v4, /device:TPU:1, one launch (start us, length us, event | category | flops | bytes accessed | tf_op | source)
XLA Modules:
  0.0 47.2 jit_solution(9844035792757974879)
XLA Ops:
  0.0 46.5 %shard_map.136 = f32[9,35,128]{2,1,0:T(8,128)S(1)} custom-call(f32[9,35,128]{2,1,0:T(8,128)} %refs_0_.1, f32[9,9,3,128]{3,2,1,0:T(4,128)} %bitcast.6, f32[9,9,4,128]{3,2,1,0:T(4,128)} %bitcast.7, f32[9,9,4,128]{3,2,1,0:T(4,128)} %bitcast.8, s32[4,128]{1,0:T(4,128)} %refs_4_.1, s32[4,128]{1,0:T(4,128)} %refs_5_.1, s32[4,128]{1,0:T(4,128)} %refs_6_.1, ...), custom_call_target="tpu_custom_call" | custom-call | tf_op jit(solution)/shard_map/pallas_call | solution.py:426
  46.5 0.7 %copy.16 = f32[9,35,128]{2,1,0:T(8,128)} copy(f32[9,35,128]{2,1,0:T(8,128)S(1)} %shard_map.136) | data formatting | bytes 322560

commit v5 on v3

--- a/solution.py
+++ b/solution.py
@@ -206,6 +206,8 @@
                 totals[i] = term if totals[i] is None else totals[i] + term
         return totals
 
+    started = []
+
     def slot_step(slot, carry, first_slot=False):
         offset = span_low & slot
         below = offset.astype(F32)
@@ -359,12 +361,13 @@
             lifted = dot(lift_w[...], face_rhs[:, cols])
             for i, q in enumerate(block):
                 fields[q] = fields[q] - lifted[0:ROWS, col(i)]
-        for copy in copies:
-            copy.wait_send()
+        started.extend(copies)
         return carry
 
-    slot_step(0, 0, first_slot=True)
-    lax.fori_loop(1, SLOTS, slot_step, 0)
+    for slot in range(SLOTS):
+        slot_step(slot, 0, first_slot=slot == 0)
+    for copy in started:
+        copy.wait_send()
     for q in range(QUANTITIES):
         out[q] = fields[q, 0:BASIS, :]
 

time: 46.6 us -> 46.3 us (level)
  no operation moved by 1% of the time
where the time goes in v5:
time: 46.3 us; the launch traced here: 46.2 us
  Pallas kernels  45.5 us (98%)
  local copies, waits for them, and re-layouts  0.68 us (1%)
    pallas_call x1, Pallas kernels, body(): pl.pallas_call(functools.partial(kernel, devices), out_shape=jax.ShapeDty...  45.5 us

profile of v5, /device:TPU:1, one launch (start us, length us, event | category | flops | bytes accessed | tf_op | source)
XLA Modules:
  0.0 46.2 jit_solution(12644065700913606425)
XLA Ops:
  0.0 45.5 %shard_map.136 = f32[9,35,128]{2,1,0:T(8,128)S(1)} custom-call(f32[9,35,128]{2,1,0:T(8,128)} %refs_0_.1, f32[9,9,3,128]{3,2,1,0:T(4,128)} %bitcast.6, f32[9,9,4,128]{3,2,1,0:T(4,128)} %bitcast.7, f32[9,9,4,128]{3,2,1,0:T(4,128)} %bitcast.8, s32[4,128]{1,0:T(4,128)} %refs_4_.1, s32[4,128]{1,0:T(4,128)} %refs_5_.1, s32[4,128]{1,0:T(4,128)} %refs_6_.1, ...), custom_call_target="tpu_custom_call" | custom-call | tf_op jit(solution)/shard_map/pallas_call | solution.py:418
  45.5 0.7 %copy.16 = f32[9,35,128]{2,1,0:T(8,128)} copy(f32[9,35,128]{2,1,0:T(8,128)S(1)} %shard_map.136) | data formatting | bytes 322560
